TPU v7x, 256 devices: a whole 4x4x8 slice. The times are simulated.
256 devices in a mesh: fsdp: 64 (over y, z, core), tensor: 4 (over x).
Axes of the slice: x: 4, y: 4, z: 8, core: 2. Of those that a mesh axis runs over, the one named last changes fastest.
Arguments:
- q_momentum: bfloat16 [16384, 16384], P('fsdp', 'tensor'), may hold values from -6 to 6
- q_weight: bfloat16 [16384, 16384], P('fsdp', 'tensor'), may hold values from -6 to 6
- q_factor: bfloat16 [16384, 128], P('tensor'), may hold values from -0.046875 to 0.046875
- kv_momentum: bfloat16 [2, 16384, 1024], P(None, 'fsdp', 'tensor'), may hold values from -6 to 6
- kv_weight: bfloat16 [2, 16384, 1024], P(None, 'fsdp', 'tensor'), may hold values from -6 to 6
- kv_factor: bfloat16 [2, 1024, 128], P(None, 'tensor'), may hold values from -0.1875 to 0.1875
Outputs:
- new_q_momentum: bfloat16 [16384, 16384], P('fsdp', 'tensor')
- new_q_weight: bfloat16 [16384, 16384], P('fsdp', 'tensor')
- new_q_factor: float32 [16384, 128], P('tensor')
- new_kv_momentum: bfloat16 [2, 16384, 1024], P(None, 'fsdp', 'tensor')
- new_kv_weight: bfloat16 [2, 16384, 1024], P(None, 'fsdp', 'tensor')
- new_kv_factor: float32 [2, 1024, 128], P(None, 'tensor')
All inputs are finite; a program needn't handle non-finite values.
Results may differ from a plain program's by a relative error of at most 0.0018.
Values sent between devices are 32-bit elements; how exact they have to be, the bound alone decides.
A program may use at most 64 MiB of HBM per device.

v0:
```python
import functools

import jax
import jax.numpy as jnp
from jax import lax
from jax.experimental import pallas as pl
from jax.experimental.pallas import tpu as pltpu
from jax.sharding import PartitionSpec as P

D = 16384
KV = 1024
R = 128
NX, NY, NZ = 4, 4, 8

feedback_rate = 0.05
learn_rate = 0.2
weight_decay = 0.1
epsilon = 1e-06

MESH = pl.DeviceIdType.MESH
HIGHEST = lax.Precision.HIGHEST
F32 = jnp.float32
BF16 = jnp.bfloat16

ROWS = 256
SUB = ROWS // NX
GROWS = 2 * R
GSH = GROWS // 8
HALF = 2304
QH = 2048
NA = 1280
NB = HALF - NA
AY, AZ = NA // NY, NA // (NY * NZ)
BZ, BY = NB // NZ, NB // (NY * NZ)
SLOT = {0: 0, 1: 1, 7: 2, 2: 3, 6: 4, 3: 5, 5: 6, 4: 7}
GROUPS = ((0, 3), (3, 2), (5, 3))
LOWER = (2, 1, 1)


VMEM_LIMIT = 59 << 20
FINISH_LIMIT = 61 << 20
LOADS = 4
ORDER = (2, 0, 1)


def coords():
    f = lax.axis_index("fsdp")
    return lax.axis_index("tensor"), f // (2 * NZ), (f // 2) % NZ, f % 2


def device(x, y, z, c):
    return ((y * NZ + z) * 2 + c, x)


def remote(src, dst, send_sem, recv_sem, dev):
    return pltpu.make_async_remote_copy(
        src_ref=src, dst_ref=dst, send_sem=send_sem, recv_sem=recv_sem,
        device_id=dev, device_id_type=MESH,
    )


def greet(peers):
    barrier = pltpu.get_barrier_semaphore()
    for dev in peers:
        pl.semaphore_signal(barrier, inc=1, device_id=dev, device_id_type=MESH)
    return barrier


def dot(a, b, ca, cb, precision=None):
    return lax.dot_general(
        a, b, (((ca,), (cb,)), ((), ())), precision=precision, preferred_element_type=F32
    )


PANEL = 8


def thirds(v):
    hi = v.astype(BF16).astype(F32)
    mid = (v - hi).astype(BF16).astype(F32)
    return hi, mid, v - hi - mid


def exact_dot(a, b, ca, cb):
    a0, a1, a2 = thirds(a)
    b0, b1, b2 = thirds(b)
    left = jnp.concatenate([a0, a0, a1, a0, a2, a1], axis=ca).astype(BF16)
    right = jnp.concatenate([b0, b1, b0, b2, b0, b1], axis=cb).astype(BF16)
    return dot(left, right, ca, cb)


def pack(g, out):
    strip = lax.broadcasted_iota(jnp.int32, (32, R), 1)
    for m in range(3):
        out[m * 32:(m + 1) * 32, :] = g[m][96:]
        out[96 + m * 32:128 + m * 32, :] = jnp.where(
            strip < 96, g[m][64:96], pltpu.roll(g[m][:32], 96, 1)
        )
    out[192:224, :] = jnp.where(strip < 64, g[0][32:64], pltpu.roll(g[1][32:64], 64, 1))
    out[224:256, :] = g[2][32:64]


def unpack(packed, out):
    strip = lax.broadcasted_iota(jnp.int32, (32, R), 1)
    lane = lax.broadcasted_iota(jnp.int32, (R, R), 1)
    row = lax.broadcasted_iota(jnp.int32, (R, R), 0)
    shared = packed[192:224, :]
    for m in range(3):
        third = packed[96 + m * 32:128 + m * 32, :]
        second = (shared, pltpu.roll(shared, 64, 1), packed[224:256, :])[m]
        low = jnp.concatenate(
            [
                jnp.where(strip < 32, pltpu.roll(third, 32, 1), 0.0),
                jnp.where(strip < 64, second, 0.0),
                jnp.where(strip < 96, third, 0.0),
                packed[m * 32:(m + 1) * 32, :],
            ],
            axis=0,
        )
        out[m] = low + jnp.where(lane // 32 < row // 32, low, 0.0).T


def inverse_factors(gram, out, work):
    lane = lax.broadcasted_iota(jnp.int32, (3, PANEL, R), 2)
    sub = lax.broadcasted_iota(jnp.int32, (3, PANEL, R), 1)

    def column(v, j):
        return jnp.broadcast_to(v[:, :, j:j + 1], (3, PANEL, R))

    unpack(gram, work)
    p = work[:, :PANEL, :]
    for base in range(0, R, PANEL):
        more = base + PANEL < R
        inside = (lane >= base) & (lane < base + PANEL)
        cols = [column(p, base + i) for i in range(PANEL)]
        p = jnp.where(inside, jnp.where(lane == sub + base, 1.0, 0.0), p)
        if more:
            after = work[:, base + PANEL:base + 2 * PANEL, :]
            after_cols = [column(after, base + i) for i in range(PANEL)]
            after = jnp.where(inside, 0.0, after)
        inv = jnp.zeros((3, PANEL, R), F32)
        for i in range(PANEL):
            r = 1.0 / cols[i][:, i:i + 1, :]
            inv = jnp.where(sub == i, r, inv)
            row = p[:, i:i + 1, :]
            mult = jnp.where(sub > i, cols[i] * r, 0.0)
            for b in range(i + 1, PANEL):
                pivot = cols[b][:, i:i + 1, :]
                cols[b] = cols[b] - mult * pivot
                if more:
                    after_cols[b] = after_cols[b] - after_cols[i] * r * pivot
            p = p - mult * row
            if more:
                after = after - after_cols[i] * r * row
        out[:, base:base + PANEL, :] = jnp.where(lane <= sub + base, p, 0.0) * lax.sqrt(inv)
        if base + 2 * PANEL < R:
            scaled = p * inv
            below = base + 2 * PANEL
            for m in range(3):
                old = jnp.where(inside[0, :1], 0.0, work[m, below:, :])
                work[m, below:, :] = old - exact_dot(scaled[m], p[m], 0, 0)[below:, :]
        if more:
            p = after


SEMS = dict(
    s_in=(2 + 2 * LOADS,), s_sw=(2,), r_sw=(2,), s_rs=(2, 3), r_rs=(2, 3), s_ra=(3,), r_ra=(3,),
    s_g=(7,), r_g=(7,), s_y=(3,), r_y=(3,), s_z=(7,), r_z=(7,), s_ga=(7,), r_ga=(7,),
    s_ay=(6,), r_ay=(6,), s_az=(7,), r_az=(7,), s_bz=(8,), r_bz=(8,), s_by=(3,), r_by=(3,),
    s_gaz=(7,), r_gaz=(7,), s_gay=(12,), r_gay=(12,), s_gby=(3,), r_gby=(3,), s_gbz=(8,), r_gbz=(8,),
    s_fa=(12,), r_fa=(12,), s_fb=(8,), r_fb=(8,), s_sz=(7,), r_sz=(7,),
    s_sy=(3,), r_sy=(3,), s_sx=(7,), r_sx=(7,), s_out=(2,),
)


def core_kernel(bq_hbm, fq_hbm, bkv_hbm, fkv_hbm, orth, proj_out, inv_row, inv_col,
                bq, fq, bkv, fkv, part, rs, raw, raw_in, gpart, grs, gy, gz, gram, linv, work,
                b_out, b_in, b_sib, acc, a_half, a_near, a_rel, a_s, a_z, b_half, b_far, b_near, b_rel, b_comb, b_s, b_y, proj, ga, gs, sz, sy, sx, *sems):
    (s_in, s_sw, r_sw, s_rs, r_rs, s_ra, r_ra, s_g, r_g, s_y, r_y, s_z, r_z, s_ga, r_ga,
     s_ay, r_ay, s_az, r_az, s_bz, r_bz, s_by, r_by,
     s_gaz, r_gaz, s_gay, r_gay, s_gby, r_gby, s_gbz, r_gbz,
     s_fa, r_fa, s_fb, r_fb, s_sz, r_sz, s_sy, r_sy, s_sx, r_sx, s_out) = sems
    x, y, z, c = coords()
    e = x * 2 + c
    o = 1 - c
    sibling = device(x, y, z, o)
    xs = [device((x + k) % NX, y, z, c) for k in (1, 2, 3)]
    es = [(e + k) % 8 for k in range(1, 8)]
    exs = [device(i // 2, y, z, i % 2) for i in es]
    ys = [device(x, (y + k) % NY, z, c) for k in (1, 2, 3)]
    zs = [device(x, y, (z + k) % NZ, c) for k in range(1, 8)]
    loads = [
        pltpu.make_async_copy(bkv_hbm, bkv, s_in.at[0]),
        pltpu.make_async_copy(fkv_hbm, fkv, s_in.at[1]),
    ]
    cut = 4096 // LOADS
    for i in range(LOADS):
        n = pl.ds(i * cut, cut)
        loads.append(pltpu.make_async_copy(bq_hbm.at[:, n], bq.at[:, n], s_in.at[2 + 2 * i]))
        loads.append(pltpu.make_async_copy(fq_hbm.at[n], fq.at[n], s_in.at[3 + 2 * i]))
    for copy in loads:
        copy.start()
    barrier = greet(exs + ys + zs)

    first = []

    def send(lo, n, sem):
        for k in (2, 1, 3):
            copy = remote(part.at[(x + k) % NX, pl.ds(lo, n)], rs.at[k - 1, pl.ds(lo, n)],
                          s_rs.at[sem, k - 1], r_rs.at[sem, k - 1], xs[k - 1])
            copy.start()
            first.append(copy)

    loads[0].wait()
    loads[1].wait()
    for m in range(2):
        product = dot(bkv[m], fkv[m], 1, 0)
        for i in range(NX):
            part[i, m] = product[i * SUB:(i + 1) * SUB]
    pl.semaphore_wait(barrier, 17)
    send(0, 2, 0)
    product = None
    for i in range(LOADS):
        loads[2 + 2 * i].wait()
        loads[3 + 2 * i].wait()
        more = dot(bq[:, i * cut:(i + 1) * cut], fq[i * cut:(i + 1) * cut, :], 1, 0)
        product = more if product is None else product + more
    for i in range(NX):
        part[i, 2] = product[i * SUB:(i + 1) * SUB]
    send(2, 1, 1)

    for i in range(QH // 256):
        cols = pl.ds(pl.multiple_of(o * QH + i * 256, 256), 256)
        b_out[:, i * 256:(i + 1) * 256] = bq[:, cols].astype(F32)
    b_out[:, QH:] = bkv[o].astype(F32)
    sends = []

    def go(copy):
        copy.start()
        sends.append(copy)
        return copy

    swap = go(remote(b_out, b_in, s_sw.at[0], r_sw.at[0], sibling))

    for copy in first:
        copy.wait_recv()
    mine = part[x] + rs[0] + rs[1] + rs[2]
    raw[x] = mine
    spread = [
        remote(raw.at[x], raw.at[x], s_ra.at[k - 1], r_ra.at[k - 1], xs[k - 1]) for k in (2, 1, 3)
    ]
    pack([exact_dot(mine[ORDER[m]], mine[ORDER[m]], 0, 0) for m in range(3)], gpart)
    scatter = [
        remote(gpart.at[pl.ds(es[k] * GSH, GSH)], grs.at[k], s_g.at[k], r_g.at[k], exs[k])
        for k in range(7)
    ]
    for copy in scatter:
        copy.start()
    total = gpart[pl.ds(e * GSH, GSH), :]
    for k in range(7):
        scatter[k].wait_recv()
        total = total + grs[k]
    gy[y] = total
    over_y = [remote(gy.at[y], gy.at[y], s_y.at[k], r_y.at[k], ys[k]) for k in range(3)]
    for copy in over_y + spread:
        copy.start()
    for copy in over_y:
        copy.wait_recv()
    gz[z] = gy[0] + gy[1] + gy[2] + gy[3]
    over_z = [remote(gz.at[z], gz.at[z], s_z.at[k], r_z.at[k], zs[k]) for k in range(7)]
    for copy in over_z:
        copy.start()
    for copy in spread:
        copy.wait_recv()
    twin = go(remote(raw, raw_in, s_sw.at[1], r_sw.at[1], sibling))
    swap.wait_recv()
    for i in range(HALF // 256):
        b_sib[:, i * 256:(i + 1) * 256] = b_in[:, i * 256:(i + 1) * 256].astype(BF16)
    for copy in over_z:
        copy.wait_recv()
    total = gz[0]
    for k in range(1, 8):
        total = total + gz[k]
    mine_rows = pl.ds(e * GSH, GSH)
    gram[mine_rows, :] = total
    gather = [
        remote(gram.at[mine_rows], gram.at[mine_rows], s_ga.at[k], r_ga.at[k], exs[k])
        for k in range(7)
    ]
    for copy in gather:
        copy.start()
    for copy in gather:
        copy.wait_recv()
    sends += first + spread + scatter + over_y + over_z + gather
    inverse_factors(gram, linv, work)
    twin.wait_recv()

    def half(rows, which, m):
        return exact_dot(linv[m], rows[:, which].reshape(ROWS, R), 1, 1).astype(BF16)

    q_own, q_sib = half(raw, ORDER[0], 0), half(raw_in, ORDER[0], 0)
    kv_own, kv_sib = half(raw, c, 1 + c), half(raw_in, c, 1 + c)

    def partial(i):
        cols = slice(i * 256, (i + 1) * 256)
        if i < QH // 256:
            own = bq[:, pl.ds(pl.multiple_of(c * QH + i * 256, 256), 256)]
            t = dot(q_own, own, 1, 0) + dot(q_sib, b_sib[:, cols], 1, 0)
        else:
            t = dot(kv_own, bkv[c], 1, 0) + dot(kv_sib, b_sib[:, cols], 1, 0)
        acc[i * 256:i * 256 + 128, :] = t[:, :128]
        acc[i * 256 + 128:i * 256 + 256, :] = t[:, 128:]

    a_order = (2, 1, 3)
    b_order = (4, 3, 5, 2, 6, 1, 7)

    def a_rows(p):
        return pl.ds(pl.multiple_of(p * AY, 8), AY)

    def b_rows(p):
        return pl.ds(pl.multiple_of(NA + p * BZ, 8), BZ)

    for i in range(NA // 256):
        partial(i)
    a_lower, a_upper = pl.ds(0, AY // 2), pl.ds(AY // 2, AY // 2)

    def a_send(src, dst, sem, hop):
        copy = remote(src, dst, s_ay.at[sem], r_ay.at[sem], device(x, (y + hop + NY) % NY, z, c))
        return go(copy)

    opposite = acc.at[a_rows((y + 2) % NY)]
    a_up, a_down = a_rows((y + 1) % NY), a_rows((y + 3) % NY)
    ah = [a_send(opposite.at[a_lower], a_half.at[0], 0, 1), a_send(opposite.at[a_upper], a_half.at[1], 1, -1)]
    an = [a_send(acc.at[a_up].at[a_upper], a_near.at[0, a_upper], 2, 1),
          a_send(acc.at[a_down].at[a_lower], a_near.at[1, a_lower], 3, -1)]
    for i in range(NA // 256, HALF // 256):
        partial(i)
    lower, upper = pl.ds(0, BZ // 2), pl.ds(BZ // 2, BZ // 2)

    def b_send(src, dst, sem, hop):
        copy = remote(src, dst, s_bz.at[sem], r_bz.at[sem], device(x, y, (z + hop + NZ) % NZ, c))
        return go(copy)

    opposite = acc.at[b_rows((z + 4) % NZ)]
    bh = [b_send(opposite.at[lower], b_half.at[0], 0, 2), b_send(opposite.at[upper], b_half.at[1], 1, -2)]
    bf = [b_send(acc.at[b_rows((z + 3) % NZ)], b_far.at[0], 2, 1),
          b_send(acc.at[b_rows((z + 5) % NZ)], b_far.at[1], 3, -1)]
    bn = [b_send(acc.at[b_rows((z + 1) % NZ)], b_near.at[0], 4, 1),
          b_send(acc.at[b_rows((z + 7) % NZ)], b_near.at[1], 5, -1)]
    for m in range(3):
        orth[m] = dot(raw[:, ORDER[m]].reshape(ROWS, R), linv[m], 1, 1, HIGHEST)

    for copy in ah:
        copy.wait_recv()
    a_rel[0] = acc[a_up, :][:AY // 2] + a_half[0]
    a_rel[1] = acc[a_down, :][AY // 2:] + a_half[1]
    an.append(a_send(a_rel.at[0], a_near.at[0, a_lower], 4, 1))
    an.append(a_send(a_rel.at[1], a_near.at[1, a_upper], 5, -1))
    for copy in bh + bf:
        copy.wait_recv()
    b_rel[0] = acc[b_rows((z + 2) % NZ), :] + b_far[0]
    b_rel[0, lower] = b_rel[0, lower] + b_half[0]
    b_rel[1] = acc[b_rows((z + 6) % NZ), :] + b_far[1]
    b_rel[1, upper] = b_rel[1, upper] + b_half[1]
    bc = [b_send(b_rel.at[0], b_comb.at[0], 6, 2), b_send(b_rel.at[1], b_comb.at[1], 7, -2)]

    for copy in an:
        copy.wait_recv()
    az = {}
    a_s[...] = acc[a_rows(y), :] + a_near[0] + a_near[1]
    for k in b_order:
        piece = pl.ds(pl.multiple_of((z + k) % NZ * AZ, 8), AZ)
        az[k] = go(remote(a_s.at[piece], a_z.at[k - 1], s_az.at[k - 1], r_az.at[k - 1], zs[k - 1]))
    for copy in bn + bc:
        copy.wait_recv()
    by = {}
    total = acc[b_rows(z), :] + b_near[0] + b_near[1] + b_comb[0] + b_comb[1]
    b_s[...] = total
    for k in a_order:
        piece = pl.ds(pl.multiple_of((y + k) % NY * BY, 8), BY)
        by[k] = go(remote(b_s.at[piece], b_y.at[k - 1], s_by.at[k - 1], r_by.at[k - 1], ys[k - 1]))

    mine = proj.at[c]
    for k in range(1, 8):
        az[k].wait_recv()
    total = a_s[pl.ds(pl.multiple_of(z * AZ, 8), AZ), :]
    for k in range(7):
        total = total + a_z[k]
    own_a_value = total
    ga[y, 0] = total
    gaz = {
        k: go(remote(ga.at[y, 0], ga.at[y, SLOT[NZ - k]], s_gaz.at[k - 1], r_gaz.at[k - 1], zs[k - 1]))
        for k in b_order[::-1]
    }
    for k in (1, 2, 3):
        by[k].wait_recv()
    total = b_s[pl.ds(pl.multiple_of(y * BY, 8), BY), :]
    for k in range(3):
        total = total + b_y[k]
    own_b = pl.ds(pl.multiple_of(NA + z * BZ + y * BY, 8), BY)
    mine[own_b, :] = total
    own_b_value = total
    gby = [go(remote(mine.at[own_b], mine.at[own_b], s_gby.at[k], r_gby.at[k], ys[k])) for k in range(3)]

    def squares(t, first_rank):
        n = t.shape[0]
        lane = lax.broadcasted_iota(jnp.int32, (n, R), 1)
        row = lax.broadcasted_iota(jnp.int32, (n, R), 0)
        full = jnp.broadcast_to(jnp.sum(t * t, axis=1, keepdims=True), (n, R))
        return jnp.sum(jnp.where(lane == (row + first_rank) % R, full, 0.0), axis=0, keepdims=True)

    row = lax.broadcasted_iota(jnp.int32, (8, R), 0)
    first_b = NA + z * BZ + y * BY
    in_q = lax.broadcasted_iota(jnp.int32, (BY, R), 0) + first_b < QH
    sz[z] = (
        jnp.where(row == 0, squares(own_a_value, y * AY + z * AZ), 0.0)
        + jnp.where(row == 0, squares(jnp.where(in_q, own_b_value, 0.0), first_b), 0.0)
        + jnp.where(row == 1 + c, squares(jnp.where(in_q, 0.0, own_b_value), first_b), 0.0)
    )
    sums = [go(remote(sz.at[z], sz.at[z], s_sz.at[k], r_sz.at[k], zs[k])) for k in range(7)]

    fa, y1, y2 = [], {}, {}

    def a_forward(back, group):
        first, n = GROUPS[group]
        block = (y - back + NY) % NY, pl.ds(first, n)
        sem = back * 3 + group
        fa.append(go(remote(ga.at[block], gs.at[block], s_fa.at[sem], r_fa.at[sem], sibling)))

    def y_send(block, first, n, sem, hop):
        ref = ga.at[block, pl.ds(first, n)]
        copy = remote(ref, ref, s_gay.at[sem], r_gay.at[sem], device(x, (y + hop + NY) % NY, z, c))
        return go(copy)

    def over_z_done(group):
        first, n = GROUPS[group]
        for rel, slot in SLOT.items():
            if rel and first <= slot < first + n:
                gaz[NZ - rel].wait_recv()
        y1[group] = [y_send(y, first, n, group * 4, 1), y_send(y, first, n, group * 4 + 1, -1)]
        a_forward(0, group)

    def round_y(group):
        first, n = GROUPS[group]
        low = LOWER[group]
        y1[group][0].wait_recv()
        one = y_send((y + NY - 1) % NY, first, low, group * 4 + 2, 1)
        y1[group][1].wait_recv()
        two = y_send((y + 1) % NY, first + low, n - low, group * 4 + 3, -1)
        y2[group] = [one, two]
        a_forward(1, group)
        a_forward(3, group)

    def opposite_done(group):
        for copy in y2[group]:
            copy.wait_recv()
        a_forward(2, group)

    def place(src, h):
        for b in range(NY):
            for rel, slot in SLOT.items():
                rows = pl.ds(pl.multiple_of(b * AY + (z + rel) % NZ * AZ, 8), AZ)
                proj[h, rows, :] = src[b, slot]

    over_z_done(0)
    for copy in gby:
        copy.wait_recv()
    block = mine.at[b_rows(z)]

    def g_send(block, part, sem, hop):
        ref = mine.at[b_rows(block)]
        ref = ref if part is None else ref.at[part]
        copy = remote(ref, ref, s_gbz.at[sem], r_gbz.at[sem], device(x, y, (z + hop + NZ) % NZ, c))
        return go(copy)

    g2 = [g_send(z, None, 0, 2), g_send(z, None, 1, -2)]
    g1 = [g_send(z, None, 2, 1), g_send(z, None, 3, -1)]
    fb = [go(remote(block, block, s_fb.at[0], r_fb.at[0], sibling))]
    over_z_done(1)
    round_y(0)
    g3, g4 = [], []

    def b_forward(back):
        block = mine.at[b_rows((z - back + NZ) % NZ)]
        fb.append(go(remote(block, block, s_fb.at[back], r_fb.at[back], sibling)))

    for k, sign in enumerate((1, -1)):
        g2[k].wait_recv()
        block = (z - 2 * sign + NZ) % NZ
        g3.append(g_send(block, None, 4 + k, sign))
        g4.append(g_send(block, (lower, upper)[k], 6 + k, 2 * sign))
        b_forward((2 * sign) % NZ)
    over_z_done(2)
    for copy in sums:
        copy.wait_recv()
    total = sz[0]
    for k in range(1, NZ):
        total = total + sz[k]
    sy[y] = total
    sums = [go(remote(sy.at[y], sy.at[y], s_sy.at[k], r_sy.at[k], ys[k])) for k in range(3)]
    round_y(1)
    for copy in sums:
        copy.wait_recv()
    sx[e] = sy[0] + sy[1] + sy[2] + sy[3]
    round_y(2)
    sums = [go(remote(sx.at[e], sx.at[e], s_sx.at[k], r_sx.at[k], exs[k])) for k in range(7)]
    for k, off in enumerate((1, 7)):
        g1[k].wait_recv()
        b_forward(off)
    for k, off in enumerate((3, 5)):
        g3[k].wait_recv()
        b_forward(off)
    opposite_done(0)
    opposite_done(1)
    for copy in g4:
        copy.wait_recv()
    b_forward(4)
    opposite_done(2)
    place(ga, c)
    outs = [pltpu.make_async_copy(mine, proj_out.at[c], s_out.at[0])]
    outs[0].start()
    for copy in sums:
        copy.wait_recv()
    total = sx[0]
    for k in range(1, 2 * NX):
        total = total + sx[k]
    scale = lax.rsqrt(total + epsilon)
    for m in range(3):
        full = jnp.broadcast_to(scale[m:m + 1], (R, R))
        inv_row[m] = full[:8]
        inv_col[m] = full.T
    for copy in fa + fb:
        copy.wait_recv()
    place(gs, o)
    outs.append(pltpu.make_async_copy(proj.at[o], proj_out.at[o], s_out.at[1]))
    outs[1].start()
    for copy in outs:
        copy.wait()
    for copy in sends:
        copy.wait_send()


VMEM = pl.BlockSpec(memory_space=pltpu.VMEM)
HBM = pl.BlockSpec(memory_space=pltpu.HBM)


def core(bq, fq, bkv, fkv):
    f32 = lambda *shape: pltpu.VMEM(shape, F32)
    return pl.pallas_call(
        core_kernel,
        out_shape=(
            jax.ShapeDtypeStruct((3, ROWS, R), F32),
            jax.ShapeDtypeStruct((2, HALF, R), F32),
            jax.ShapeDtypeStruct((3, 8, R), F32),
            jax.ShapeDtypeStruct((3, R, R), F32),
        ),
        in_specs=[HBM] * 4,
        out_specs=(VMEM, HBM, VMEM, VMEM),
        scratch_shapes=[
            pltpu.VMEM((ROWS, 4096), BF16),
            pltpu.VMEM((4096, R), BF16),
            pltpu.VMEM((2, ROWS, 256), BF16),
            pltpu.VMEM((2, 256, R), BF16),
            f32(NX, 3, SUB, R), f32(3, 3, SUB, R), f32(NX, 3, SUB, R), f32(NX, 3, SUB, R),
            f32(GROWS, R), f32(7, GSH, R), f32(NY, GSH, R), f32(NZ, GSH, R),
            f32(GROWS, R), f32(3, R, R), f32(3, R, R),
            f32(ROWS, HALF), f32(ROWS, HALF), pltpu.VMEM((ROWS, HALF), BF16), f32(HALF, R),
            f32(2, AY // 2, R), f32(2, AY, R), f32(2, AY // 2, R), f32(AY, R), f32(7, AZ, R),
            f32(2, BZ // 2, R), f32(2, BZ, R), f32(2, BZ, R), f32(2, BZ, R), f32(2, BZ, R),
            f32(BZ, R), f32(3, BY, R),
            f32(2, HALF, R), f32(NY, NZ, AZ, R), f32(NY, NZ, AZ, R), f32(NZ, 8, R), f32(NY, 8, R), f32(2 * NX, 8, R),
            *[pltpu.SemaphoreType.DMA(shape) for shape in SEMS.values()],
        ],
        compiler_params=pltpu.CompilerParams(
            collective_id=1, has_side_effects=True, vmem_limit_bytes=VMEM_LIMIT
        ),
        name="core",
    )(bq, fq, bkv, fkv)


def split(v):
    hi = v.astype(BF16)
    return hi, (v - hi.astype(F32)).astype(BF16)


def wide(v):
    hi, lo = split(v)
    return jnp.concatenate([hi, hi, lo], axis=1)


BLOCK = 1024
AHEAD = 3
CHUNKS = 4096 // BLOCK
Q_SCALE = learn_rate * (D * D / R) ** 0.5
KV_SCALE = learn_rate * (D * KV / R) ** 0.5
KEEP = 1.0 - learn_rate * weight_decay


def finish_kernel(orth_hbm, inv_row_hbm, inv_col_hbm, t_hbm, bq_hbm, wq_hbm, bkv_hbm, wkv_hbm,
                  mom_q_hbm, w_q_hbm, f_q_hbm, mom_kv_hbm, w_kv_hbm, f_kv_hbm,
                  orth, inv_row, inv_col, t_ref, bq, wq, bkv, wkv,
                  mom_q, w_q, f_q, mom_kv, w_kv, f_kv, s_head, s_in, s_out):
    def load(src, dst, sem):
        copy = pltpu.make_async_copy(src, dst, sem)
        copy.start()
        return copy

    head = [
        load(src, dst, s_head.at[i])
        for i, (src, dst) in enumerate(
            ((orth_hbm, orth), (inv_row_hbm, inv_row), (inv_col_hbm, inv_col))
        )
    ]
    loads = {}

    def fetch(i):
        if i < CHUNKS:
            h, cols = i // (CHUNKS // 2), pl.ds(i * BLOCK, BLOCK)
            rows = pl.ds(i % (CHUNKS // 2) * BLOCK, BLOCK)
            pairs = (
                (t_hbm.at[h, rows], t_ref.at[h, rows]),
                (bq_hbm.at[:, cols], bq.at[:, cols]),
                (wq_hbm.at[:, cols], wq.at[:, cols]),
            )
        elif i == CHUNKS:
            rows = pl.ds(QH, HALF - QH)
            pairs = ((t_hbm.at[:, rows], t_ref.at[:, rows]), (bkv_hbm, bkv), (wkv_hbm, wkv))
        else:
            return
        loads[i] = [load(src, dst, s_in.at[i, k]) for k, (src, dst) in enumerate(pairs)]

    for i in range(AHEAD):
        fetch(i)
    for copy in head:
        copy.wait()

    def lefts(m, scale):
        v = orth[m]
        return jnp.concatenate(
            [wide(v * -feedback_rate), wide(v * (inv_row[m, :1] * -scale))], axis=0
        )

    def products(t, a):
        hi, lo = split(jnp.concatenate([t[:R], t[R:]], axis=1))
        t = jnp.concatenate([hi, lo, hi], axis=0)
        both = dot(a, t, 1, 0)
        return both[:ROWS], both[ROWS:]

    stores = []

    def store(src, dst, sem):
        stores.append(load(src, dst, sem))

    a = lefts(0, Q_SCALE)
    for i in range(CHUNKS):
        for copy in loads[i]:
            copy.wait()
        fetch(i + AHEAD)
        h, base = i // (CHUNKS // 2), i % (CHUNKS // 2) * BLOCK
        for j in range(0, BLOCK, 2 * R):
            t = t_ref[h, base + j:base + j + 2 * R, :]
            cols = slice(i * BLOCK + j, i * BLOCK + j + 2 * R)
            p, u = products(t, a)
            mom_q[:, cols] = (bq[:, cols].astype(F32) + p).astype(BF16)
            w_q[:, cols] = (KEEP * wq[:, cols].astype(F32) + u).astype(BF16)
            f_q[i * BLOCK + j:i * BLOCK + j + R, :] = (t[:R] * inv_col[0]).T
            f_q[i * BLOCK + j + R:i * BLOCK + j + 2 * R, :] = (t[R:] * inv_col[0]).T
        cols = pl.ds(i * BLOCK, BLOCK)
        store(mom_q.at[:, cols], mom_q_hbm.at[:, cols], s_out.at[i, 0])
        store(w_q.at[:, cols], w_q_hbm.at[:, cols], s_out.at[i, 1])
        store(f_q.at[cols], f_q_hbm.at[cols], s_out.at[i, 2])
    for copy in loads[CHUNKS]:
        copy.wait()
    for m in range(2):
        a = lefts(m + 1, KV_SCALE)
        t = t_ref[m, QH:, :]
        p, u = products(t, a)
        mom_kv[m] = (bkv[m].astype(F32) + p).astype(BF16)
        w_kv[m] = (KEEP * wkv[m].astype(F32) + u).astype(BF16)
        f_kv[m, :R, :] = (t[:R] * inv_col[m + 1]).T
        f_kv[m, R:, :] = (t[R:] * inv_col[m + 1]).T
    store(mom_kv, mom_kv_hbm, s_out.at[CHUNKS, 0])
    store(w_kv, w_kv_hbm, s_out.at[CHUNKS, 1])
    store(f_kv, f_kv_hbm, s_out.at[CHUNKS, 2])
    for copy in stores:
        copy.wait()


def finish(orth, proj, inv_row, inv_col, bq, wq, bkv, wkv):
    outs = (
        ((ROWS, 4096), BF16), ((ROWS, 4096), BF16), ((4096, R), F32),
        ((2, ROWS, 256), BF16), ((2, ROWS, 256), BF16), ((2, 256, R), F32),
    )
    args = (orth, inv_row, inv_col, proj, bq, wq, bkv, wkv)
    return pl.pallas_call(
        finish_kernel,
        out_shape=tuple(jax.ShapeDtypeStruct(*out) for out in outs),
        in_specs=[HBM] * 8,
        out_specs=(HBM,) * 6,
        scratch_shapes=[
            *[pltpu.VMEM(arg.shape, arg.dtype) for arg in args],
            *[pltpu.VMEM(*out) for out in outs],
            pltpu.SemaphoreType.DMA((3,)),
            pltpu.SemaphoreType.DMA((CHUNKS + 1, 3)),
            pltpu.SemaphoreType.DMA((CHUNKS + 1, 3)),
        ],
        compiler_params=pltpu.CompilerParams(vmem_limit_bytes=FINISH_LIMIT),
        name="finish",
    )(*args)


def local(q_momentum, q_weight, q_factor, kv_momentum, kv_weight, kv_factor):
    orth, proj, inv_row, inv_col = core(q_momentum, q_factor, kv_momentum, kv_factor)
    return finish(orth, proj, inv_row, inv_col, q_momentum, q_weight, kv_momentum, kv_weight)


def solution(mesh):
    specs = (
        P("fsdp", "tensor"),
        P("fsdp", "tensor"),
        P("tensor", None),
        P(None, "fsdp", "tensor"),
        P(None, "fsdp", "tensor"),
        P(None, "tensor", None),
    )
    return jax.shard_map(local, mesh=mesh, in_specs=specs, out_specs=specs, check_vma=False)
```

profile of v0, /device:TPU:1, one launch (start us, length us, event | category | flops | bytes accessed | tf_op | source)
XLA Modules:
  0.0 85.7 jit_solution(6950654112705745930)
XLA Ops:
  0.6 78.3 %core.1 = (f32[3,256,128]{2,1,0:T(8,128)}, f32[2,2304,128]{2,1,0:T(8,128)}, f32[3,8,128]{2,1,0:T(8,128)}, f32[3,128,128]{2,1,0:T(8,128)}) custom-call(bf16[256,4096]{1,0:T(8,128)(2,1)} %bq_hbm.3, bf16[4096,128]{1,0:T(8,128)(2,1)} %fq_hbm.1, bf16[2,256,256]{2,1,0:T(8,128)(2,1)} %bkv_hbm.3, bf16[2,256,128]{2,1,0:T(8,128)(2,1)} %fkv_hbm.1), custom_call_target="tpu_custom_call" | custom-call | tf_op jit(solution)/shard_map/core/pallas_call | solution.py:549
  78.9 6.8 %finish.1 = (bf16[256,4096]{1,0:T(8,128)(2,1)}, bf16[256,4096]{1,0:T(8,128)(2,1)}, f32[4096,128]{1,0:T(8,128)}, bf16[2,256,256]{2,1,0:T(8,128)(2,1)}, bf16[2,256...) custom-call(f32[3,256,128]{2,1,0:T(8,128)} %get-tuple-element.10.orth_hbm, f32[3,8,128]{2,1,0:T(8,128)} %get-tuple-element.11.inv_row_hbm, ...), custom_call_target="tpu_custom_call" | custom-call | tf_op jit(solution)/shard_map/finish/pallas_call | solution.py:695
where the time goes:
time: 85.8 us; the launch traced here: 85.7 us
  Pallas kernels  85.1 us (99%)
    pallas_call x1, Pallas kernels, core(): pl.pallas_call(core_kernel, out_shape=(jax.ShapeDtypeStruct((3, ROWS, R),...  78.3 us
    pallas_call x1, Pallas kernels, finish(): pl.pallas_call(finish_kernel, out_shape=tuple((jax.ShapeDtypeStruct(*out)...  6.79 us

commit v1 on v0

--- a/solution.py
+++ b/solution.py
@@ -169,13 +169,13 @@
     s_ay=(6,), r_ay=(6,), s_az=(7,), r_az=(7,), s_bz=(8,), r_bz=(8,), s_by=(3,), r_by=(3,),
     s_gaz=(7,), r_gaz=(7,), s_gay=(12,), r_gay=(12,), s_gby=(3,), r_gby=(3,), s_gbz=(8,), r_gbz=(8,),
     s_fa=(12,), r_fa=(12,), s_fb=(8,), r_fb=(8,), s_sz=(7,), r_sz=(7,),
-    s_sy=(3,), r_sy=(3,), s_sx=(7,), r_sx=(7,), s_out=(2,),
+    s_sy=(3,), r_sy=(3,), s_sx=(7,), r_sx=(7,), s_out=(4,),
 )
 
 
-def core_kernel(bq_hbm, fq_hbm, bkv_hbm, fkv_hbm, orth, proj_out, inv_row, inv_col,
+def core_kernel(bq_hbm, fq_hbm, bkv_hbm, fkv_hbm, orth_out, proj_out, inv_row,
                 bq, fq, bkv, fkv, part, rs, raw, raw_in, gpart, grs, gy, gz, gram, linv, work,
-                b_out, b_in, b_sib, acc, a_half, a_near, a_rel, a_s, a_z, b_half, b_far, b_near, b_rel, b_comb, b_s, b_y, proj, ga, gs, sz, sy, sx, *sems):
+                b_out, b_in, b_sib, acc, a_half, a_near, a_rel, a_s, a_z, b_half, b_far, b_near, b_rel, b_comb, b_s, b_y, orth, proj, ga, gs, sz, sy, sx, *sems):
     (s_in, s_sw, r_sw, s_rs, r_rs, s_ra, r_ra, s_g, r_g, s_y, r_y, s_z, r_z, s_ga, r_ga,
      s_ay, r_ay, s_az, r_az, s_bz, r_bz, s_by, r_by,
      s_gaz, r_gaz, s_gay, r_gay, s_gby, r_gby, s_gbz, r_gbz,
@@ -348,7 +348,9 @@
     bn = [b_send(acc.at[b_rows((z + 1) % NZ)], b_near.at[0], 4, 1),
           b_send(acc.at[b_rows((z + 7) % NZ)], b_near.at[1], 5, -1)]
     for m in range(3):
-        orth[m] = dot(raw[:, ORDER[m]].reshape(ROWS, R), linv[m], 1, 1, HIGHEST)
+        orth[m] = exact_dot(raw[:, ORDER[m]].reshape(ROWS, R), linv[m], 1, 1)
+    outs = [pltpu.make_async_copy(orth, orth_out, s_out.at[0])]
+    outs[0].start()
 
     for copy in ah:
         copy.wait_recv()
@@ -477,7 +479,6 @@
     g1 = [g_send(z, None, 2, 1), g_send(z, None, 3, -1)]
     fb = [go(remote(block, block, s_fb.at[0], r_fb.at[0], sibling))]
     over_z_done(1)
-    round_y(0)
     g3, g4 = [], []
 
     def b_forward(back):
@@ -490,6 +491,7 @@
         g3.append(g_send(block, None, 4 + k, sign))
         g4.append(g_send(block, (lower, upper)[k], 6 + k, 2 * sign))
         b_forward((2 * sign) % NZ)
+    round_y(0)
     over_z_done(2)
     for copy in sums:
         copy.wait_recv()
@@ -517,8 +519,14 @@
     b_forward(4)
     opposite_done(2)
     place(ga, c)
-    outs = [pltpu.make_async_copy(mine, proj_out.at[c], s_out.at[0])]
-    outs[0].start()
+
+    def write(h, first, n, sem):
+        rows = pl.ds(first, n)
+        copy = pltpu.make_async_copy(proj.at[h, rows], proj_out.at[h, rows], s_out.at[sem])
+        copy.start()
+        outs.append(copy)
+
+    write(c, 0, HALF, 1)
     for copy in sums:
         copy.wait_recv()
     total = sx[0]
@@ -526,14 +534,14 @@
         total = total + sx[k]
     scale = lax.rsqrt(total + epsilon)
     for m in range(3):
-        full = jnp.broadcast_to(scale[m:m + 1], (R, R))
-        inv_row[m] = full[:8]
-        inv_col[m] = full.T
-    for copy in fa + fb:
+        inv_row[m] = jnp.broadcast_to(scale[m:m + 1], (8, R))
+    for copy in fb:
+        copy.wait_recv()
+    write(o, NA, NB, 2)
+    for copy in fa:
         copy.wait_recv()
     place(gs, o)
-    outs.append(pltpu.make_async_copy(proj.at[o], proj_out.at[o], s_out.at[1]))
-    outs[1].start()
+    write(o, 0, NA, 3)
     for copy in outs:
         copy.wait()
     for copy in sends:
@@ -552,10 +560,9 @@
             jax.ShapeDtypeStruct((3, ROWS, R), F32),
             jax.ShapeDtypeStruct((2, HALF, R), F32),
             jax.ShapeDtypeStruct((3, 8, R), F32),
-            jax.ShapeDtypeStruct((3, R, R), F32),
         ),
         in_specs=[HBM] * 4,
-        out_specs=(VMEM, HBM, VMEM, VMEM),
+        out_specs=(HBM, HBM, VMEM),
         scratch_shapes=[
             pltpu.VMEM((ROWS, 4096), BF16),
             pltpu.VMEM((4096, R), BF16),
@@ -568,7 +575,7 @@
             f32(2, AY // 2, R), f32(2, AY, R), f32(2, AY // 2, R), f32(AY, R), f32(7, AZ, R),
             f32(2, BZ // 2, R), f32(2, BZ, R), f32(2, BZ, R), f32(2, BZ, R), f32(2, BZ, R),
             f32(BZ, R), f32(3, BY, R),
-            f32(2, HALF, R), f32(NY, NZ, AZ, R), f32(NY, NZ, AZ, R), f32(NZ, 8, R), f32(NY, 8, R), f32(2 * NX, 8, R),
+            f32(3, ROWS, R), f32(2, HALF, R), f32(NY, NZ, AZ, R), f32(NY, NZ, AZ, R), f32(NZ, 8, R), f32(NY, 8, R), f32(2 * NX, 8, R),
             *[pltpu.SemaphoreType.DMA(shape) for shape in SEMS.values()],
         ],
         compiler_params=pltpu.CompilerParams(
@@ -596,9 +603,9 @@
 KEEP = 1.0 - learn_rate * weight_decay
 
 
-def finish_kernel(orth_hbm, inv_row_hbm, inv_col_hbm, t_hbm, bq_hbm, wq_hbm, bkv_hbm, wkv_hbm,
+def finish_kernel(orth_hbm, inv_row_hbm, t_hbm, bq_hbm, wq_hbm, bkv_hbm, wkv_hbm,
                   mom_q_hbm, w_q_hbm, f_q_hbm, mom_kv_hbm, w_kv_hbm, f_kv_hbm,
-                  orth, inv_row, inv_col, t_ref, bq, wq, bkv, wkv,
+                  orth, inv_row, t_ref, bq, wq, bkv, wkv,
                   mom_q, w_q, f_q, mom_kv, w_kv, f_kv, s_head, s_in, s_out):
     def load(src, dst, sem):
         copy = pltpu.make_async_copy(src, dst, sem)
@@ -608,7 +615,7 @@
     head = [
         load(src, dst, s_head.at[i])
         for i, (src, dst) in enumerate(
-            ((orth_hbm, orth), (inv_row_hbm, inv_row), (inv_col_hbm, inv_col))
+            ((orth_hbm, orth), (inv_row_hbm, inv_row))
         )
     ]
     loads = {}
@@ -663,8 +670,8 @@
             p, u = products(t, a)
             mom_q[:, cols] = (bq[:, cols].astype(F32) + p).astype(BF16)
             w_q[:, cols] = (KEEP * wq[:, cols].astype(F32) + u).astype(BF16)
-            f_q[i * BLOCK + j:i * BLOCK + j + R, :] = (t[:R] * inv_col[0]).T
-            f_q[i * BLOCK + j + R:i * BLOCK + j + 2 * R, :] = (t[R:] * inv_col[0]).T
+            f_q[i * BLOCK + j:i * BLOCK + j + R, :] = t[:R].T * inv_row[0, :1]
+            f_q[i * BLOCK + j + R:i * BLOCK + j + 2 * R, :] = t[R:].T * inv_row[0, :1]
         cols = pl.ds(i * BLOCK, BLOCK)
         store(mom_q.at[:, cols], mom_q_hbm.at[:, cols], s_out.at[i, 0])
         store(w_q.at[:, cols], w_q_hbm.at[:, cols], s_out.at[i, 1])
@@ -677,8 +684,8 @@
         p, u = products(t, a)
         mom_kv[m] = (bkv[m].astype(F32) + p).astype(BF16)
         w_kv[m] = (KEEP * wkv[m].astype(F32) + u).astype(BF16)
-        f_kv[m, :R, :] = (t[:R] * inv_col[m + 1]).T
-        f_kv[m, R:, :] = (t[R:] * inv_col[m + 1]).T
+        f_kv[m, :R, :] = t[:R].T * inv_row[m + 1, :1]
+        f_kv[m, R:, :] = t[R:].T * inv_row[m + 1, :1]
     store(mom_kv, mom_kv_hbm, s_out.at[CHUNKS, 0])
     store(w_kv, w_kv_hbm, s_out.at[CHUNKS, 1])
     store(f_kv, f_kv_hbm, s_out.at[CHUNKS, 2])
@@ -686,21 +693,21 @@
         copy.wait()
 
 
-def finish(orth, proj, inv_row, inv_col, bq, wq, bkv, wkv):
+def finish(orth, proj, inv_row, bq, wq, bkv, wkv):
     outs = (
         ((ROWS, 4096), BF16), ((ROWS, 4096), BF16), ((4096, R), F32),
         ((2, ROWS, 256), BF16), ((2, ROWS, 256), BF16), ((2, 256, R), F32),
     )
-    args = (orth, inv_row, inv_col, proj, bq, wq, bkv, wkv)
+    args = (orth, inv_row, proj, bq, wq, bkv, wkv)
     return pl.pallas_call(
         finish_kernel,
         out_shape=tuple(jax.ShapeDtypeStruct(*out) for out in outs),
-        in_specs=[HBM] * 8,
+        in_specs=[HBM] * 7,
         out_specs=(HBM,) * 6,
         scratch_shapes=[
             *[pltpu.VMEM(arg.shape, arg.dtype) for arg in args],
             *[pltpu.VMEM(*out) for out in outs],
-            pltpu.SemaphoreType.DMA((3,)),
+            pltpu.SemaphoreType.DMA((2,)),
             pltpu.SemaphoreType.DMA((CHUNKS + 1, 3)),
             pltpu.SemaphoreType.DMA((CHUNKS + 1, 3)),
         ],
@@ -710,8 +717,8 @@
 
 
 def local(q_momentum, q_weight, q_factor, kv_momentum, kv_weight, kv_factor):
-    orth, proj, inv_row, inv_col = core(q_momentum, q_factor, kv_momentum, kv_factor)
-    return finish(orth, proj, inv_row, inv_col, q_momentum, q_weight, kv_momentum, kv_weight)
+    orth, proj, inv_row = core(q_momentum, q_factor, kv_momentum, kv_factor)
+    return finish(orth, proj, inv_row, q_momentum, q_weight, kv_momentum, kv_weight)
 
 
 def solution(mesh):

time: 85.8 us -> 85.8 us (level)
  no operation moved by 1% of the time
where the time goes in v1:
time: 85.8 us; the launch traced here: 85.7 us
  Pallas kernels  85.1 us (99%)
    pallas_call x1, Pallas kernels, core(): pl.pallas_call(core_kernel, out_shape=(jax.ShapeDtypeStruct((3, ROWS, R),...  78.4 us
    pallas_call x1, Pallas kernels, finish(): pl.pallas_call(finish_kernel, out_shape=tuple((jax.ShapeDtypeStruct(*out)...  6.62 us

profile of v1, /device:TPU:1, one launch (start us, length us, event | category | flops | bytes accessed | tf_op | source)
XLA Modules:
  0.0 85.7 jit_solution(4142081576386253063)
XLA Ops:
  0.6 78.4 %core.1 = (f32[3,256,128]{2,1,0:T(8,128)}, f32[2,2304,128]{2,1,0:T(8,128)}, f32[3,8,128]{2,1,0:T(8,128)}) custom-call(bf16[256,4096]{1,0:T(8,128)(2,1)} %bq_hbm.3, bf16[4096,128]{1,0:T(8,128)(2,1)} %fq_hbm.1, bf16[2,256,256]{2,1,0:T(8,128)(2,1)} %bkv_hbm.3, bf16[2,256,128]{2,1,0:T(8,128)(2,1)} %fkv_hbm.1), custom_call_target="tpu_custom_call" | custom-call | tf_op jit(solution)/shard_map/core/pallas_call | solution.py:557
  79.1 6.6 %finish.1 = (bf16[256,4096]{1,0:T(8,128)(2,1)}, bf16[256,4096]{1,0:T(8,128)(2,1)}, f32[4096,128]{1,0:T(8,128)}, bf16[2,256,256]{2,1,0:T(8,128)(2,1)}, bf16[2,256...) custom-call(f32[3,256,128]{2,1,0:T(8,128)} %get-tuple-element.9.orth_hbm, f32[3,8,128]{2,1,0:T(8,128)} %get-tuple-element.10.inv_row_hbm, ...), custom_call_target="tpu_custom_call" | custom-call | tf_op jit(solution)/shard_map/finish/pallas_call | solution.py:702
